TPU v7x, 32 devices: a whole 2x2x4 slice. The times are simulated.
32 devices in a mesh: parts: 2 (over x), gx: 4 (over y, core), gy: 4 (over z).
Axes of the slice: x: 2, y: 2, z: 4, core: 2. Of those that a mesh axis runs over, the one named last changes fastest.
Arguments:
- forcing_right_side: float32 [32, 32, 1024], P(('parts', 'gx'), 'gy'), parts along dimension 0, may hold values from -18 to 18
- earlier_warmth: float32 [32, 32, 1024], P(('parts', 'gx'), 'gy'), parts along dimension 0, may hold values from 0 to 2
- matter_condition: int32 [32, 32, 1024], P(('parts', 'gx'), 'gy'), parts along dimension 0, may hold values from 0 to 2
- compressed_slot_number: int32 [32, 32, 1024], P(('parts', 'gx'), 'gy'), parts along dimension 0, may hold values from 0 to 127
- normal_draw_factor: float32 [32, 32, 1024], P(('parts', 'gx'), 'gy'), parts along dimension 0, may hold values from -6 to 6
Outputs:
- solution: float32 [32, 32, 1024], P(('parts', 'gx'), 'gy'), parts along dimension 0
- residual: float32 [32, 32, 1024], P(('parts', 'gx'), 'gy'), parts along dimension 0
There are 2 independent parts, one for each index of `parts`. A program takes and returns all parts, laid end to end along the dimension named above; each array names one. Nothing has to cross between parts.
Inputs may be any that keep to these rules, and one draw needn't show every extreme that they name: `matter_condition`: phase labels the cell as powder, solid or liquid. `compressed_slot_number`: each cell's row of the sketch.
All inputs are finite; a program needn't handle non-finite values.
Results may differ from a plain program's by a relative error of at most 0.0003.
Values sent between devices are 32-bit elements; how exact they have to be, the bound alone decides.
No kernel may reach another device: no remote copies, remote signals or barrier semaphores. Data moves between devices by JAX's collectives and lax.ppermute only.
A program may use at most 64 MiB of HBM per device.

v0:
```python
import math

import jax
import jax.numpy as jnp
from jax import lax
from jax.sharding import PartitionSpec as P

BASIS = 2
SKETCH = 128


epsilon = 1e-06
highest = lax.Precision.HIGHEST


def padded_2(block, sides, width):
    for axis, dim in sides:
        count = lax.axis_size(axis)
        forward = [(i, i + 1) for i in range(count - 1)]
        backward = [(target, source) for source, target in forward]
        low = lax.ppermute(
            lax.slice_in_dim(block, block.shape[dim] - width, None, axis=dim), axis, forward
        )
        high = lax.ppermute(lax.slice_in_dim(block, 0, width, axis=dim), axis, backward)
        block = jnp.concatenate([low, block, high], axis=dim)
    return block


def medium_traits(earlier_warmth, matter_condition):
    datum_offset = jnp.where(
        matter_condition == 0, 0.2, jnp.where(matter_condition == 1, 1.0, 0.6)
    ).astype(jnp.float32)
    spreading_rate = datum_offset * (0.5 + earlier_warmth)
    volumetric_retention = jnp.where(
        matter_condition == 0, 1.0, jnp.where(matter_condition == 1, 2.0, 1.5)
    ).astype(jnp.float32)
    return (spreading_rate, volumetric_retention)


def harmonic(first, second):
    return 2.0 * first * second / (first + second)


def beside_all(padded, field):
    depth = jnp.pad(field, ((0, 0), (0, 0), (1, 1)))
    return [
        padded[2:, 1:-1],
        padded[:-2, 1:-1],
        padded[1:-1, 2:],
        padded[1:-1, :-2],
        depth[:, :, 2:],
        depth[:, :, :-2],
    ]


def sketch_local(field, compressed_slot_number, normal_draw_factor):
    weighted = (normal_draw_factor * field).reshape(-1)
    row_ids = compressed_slot_number.reshape(-1)
    cells = weighted.shape[0]
    block_size = math.gcd(cells, 8192)
    block_count = cells // block_size
    weighted = weighted.reshape(block_count, block_size)
    row_ids = row_ids.reshape(block_count, block_size)
    slots = lax.broadcasted_iota(jnp.int32, (1, SKETCH), 1)

    def add_block(totals, block_pair):
        block_vals, block_rows = block_pair
        onehot = (block_rows[:, None] == slots).astype(jnp.float32)
        return (totals + jnp.dot(block_vals, onehot, precision=highest), None)

    totals, unused = lax.scan(add_block, jnp.zeros((SKETCH,), jnp.float32), (weighted, row_ids))
    return totals


def solve_small(hess, scale_norm):
    width_count = hess.shape[1]
    gram_matrix = jnp.dot(hess.T, hess, precision=highest)
    target = scale_norm * hess[0]
    factor = jnp.linalg.cholesky(gram_matrix)
    forward = []
    for row_a in range(width_count):
        partial_sum = target[row_a]
        for prior in range(row_a):
            partial_sum = partial_sum - factor[row_a, prior] * forward[prior]
        forward.append(partial_sum / factor[row_a, row_a])
    backward = [None] * width_count
    for row_a in reversed(range(width_count)):
        partial_sum = forward[row_a]
        for later in range(row_a + 1, width_count):
            partial_sum = partial_sum - factor[later, row_a] * backward[later]
        backward[row_a] = partial_sum / factor[row_a, row_a]
    return backward


def body(
    forcing_right_side, earlier_warmth, matter_condition, compressed_slot_number, normal_draw_factor
):
    spreading_rate, volumetric_retention = medium_traits(earlier_warmth, matter_condition)
    padded_cond = padded_2(spreading_rate, (("gx", 0), ("gy", 1)), 1)
    links = [harmonic(spreading_rate, other) for other in beside_all(padded_cond, spreading_rate)]

    def operate(field):
        padded = padded_2(field, (("gx", 0), ("gy", 1)), 1)
        result = volumetric_retention * field
        for conductance, neighbour in zip(links, beside_all(padded, field)):
            result = result + conductance * (field - neighbour)
        return result

    def sketch_sum(field):
        return lax.psum(
            sketch_local(field, compressed_slot_number, normal_draw_factor), ("gx", "gy")
        )

    solution = jnp.zeros_like(forcing_right_side)
    residual = forcing_right_side
    sketched = sketch_sum(residual)
    scale_norm = jnp.sqrt(jnp.sum(sketched * sketched) + epsilon)
    basis_list = [residual / scale_norm]
    sketch_list = [sketched / scale_norm]
    image_list = []
    columns = []
    for column in range(BASIS):
        images = operate(basis_list[column])
        image_list.append(images)
        image_sketch = sketch_sum(images)
        stacked = jnp.stack(sketch_list, axis=1)
        coeffs = jnp.dot(stacked.T, image_sketch, precision=highest)
        reduced = images
        for prior in range(column + 1):
            reduced = reduced - coeffs[prior] * basis_list[prior]
        remainder = image_sketch - jnp.dot(stacked, coeffs, precision=highest)
        norm_next = jnp.sqrt(jnp.sum(remainder * remainder) + epsilon)
        columns.append(
            jnp.concatenate(
                [coeffs, norm_next[None], jnp.zeros((BASIS - column - 1,), jnp.float32)]
            )
        )
        if column + 1 < BASIS:
            basis_list.append(reduced / norm_next)
            sketch_list.append(remainder / norm_next)
    hess = jnp.stack(columns, axis=1)
    weights = solve_small(hess, scale_norm)
    for prior in range(BASIS):
        solution = solution + weights[prior] * basis_list[prior]
    residual = forcing_right_side - operate(solution)
    return (solution, residual)


def solution(mesh):
    return jax.shard_map(
        body,
        mesh=mesh,
        in_specs=(
            P(("parts", "gx"), "gy", None),
            P(("parts", "gx"), "gy", None),
            P(("parts", "gx"), "gy", None),
            P(("parts", "gx"), "gy", None),
            P(("parts", "gx"), "gy", None),
        ),
        out_specs=(P(("parts", "gx"), "gy", None), P(("parts", "gx"), "gy", None)),
        check_vma=False,
    )
```

profile of v0, /device:TPU:0, one launch (start us, length us, event | category | flops | bytes accessed | tf_op | source)
XLA Modules:
  0.0 187.5 jit_solution(5906491994559464097)
XLA Ops:
  1.8 7.4 %while.33 = (s32[]{:T(128)}, f32[128]{0:T(128)S(1)}, f32[4,8192]{1,0:T(4,128)S(1)}, s32[4,8192]{1,0:T(4,128)S(1)}, s32[]{:T(128)}, /*index=5*/s32[]{:T(128)}) while((s32[]{:T(128)}, f32[128]{0:T(128)S(1)}, f32[4,8192]{1,0:T(4,128)S(1)}, s32[4,8192]{1,0:T(4,128)S(1)}, s32[]{:T(128)}, /*index=5*/s32[]{:T(128)}) %tuple.88), condition=%wide.region_1.2_spmd.clone, body=%wide.region_0.1_spmd.clone.sunk | while | flops 13631747 | bytes 132183 | solution.py:71
  1.9 1.8 fusion.118
  3.8 1.8 fusion.118
  5.6 1.8 fusion.118
  7.5 1.8 fusion.118
  9.3 35.2 %psum.21 = f32[128]{0:T(128)S(1)} all-reduce(f32[128]{0:T(128)S(1)} %get-tuple-element.83), channel_id=1, replica_groups=mesh['parts'=2,'gx'=4,'gy'=4] {'gx','gy'}, use_global_device_ids=true, to_apply=%region_2.3 | all-reduce | flops 128 | bytes 1024 | tf_op jit(solution)/shard_map/psum | solution.py:110
  47.3 3.0 %collective-permute-start.3 = (f32[1,8,1024]{2,1,0:T(8,128)S(1)}, f32[1,8,1024]{2,1,0:T(8,128)S(1)}, u32[]{:S(2)}, u32[]{:S(2)}) collective-permute-start(f32[1,8,1024]{2,1,0:T(8,128)S(1)} %get-tuple-element.182), channel_id=1, source_target_pairs={{0,4},{4,8},{8,12},{1,5},{5,9},{9,13},{2,6},{6,10},{10,14},{3,7},{... | collective-permute-start | bytes 98312 | tf_op jit(solution)/shard_map/ppermute | solution.py:21
  51.7 3.0 %collective-permute-start.2 = (f32[1,8,1024]{2,1,0:T(8,128)S(1)}, f32[1,8,1024]{2,1,0:T(8,128)S(1)}, u32[]{:S(2)}, u32[]{:S(2)}) collective-permute-start(f32[1,8,1024]{2,1,0:T(8,128)S(1)} %get-tuple-element.180), channel_id=1, source_target_pairs={{0,4},{4,8},{8,12},{1,5},{5,9},{9,13},{2,6},{6,10},{10,14},{3,7},{... | collective-permute-start | bytes 98312 | tf_op jit(solution)/shard_map/ppermute | solution.py:21
  56.1 4.5 %collective-permute-start.7 = (f32[6,1,1024]{2,1,0:T(1,128)S(1)}, f32[6,1,1024]{2,1,0:T(1,128)S(1)}, u32[]{:S(2)}, u32[]{:S(2)}) collective-permute-start(f32[6,1,1024]{2,1,0:T(1,128)S(1)} %get-tuple-element.175), channel_id=1, source_target_pairs={{0,1},{1,2},{2,3},{4,5},{5,6},{6,7},{8,9},{9,10},{10,11},{12,13},{... | collective-permute-start | bytes 73736 | tf_op jit(solution)/shard_map/ppermute | solution.py:21
  62.0 4.5 %collective-permute-start.6 = (f32[6,1,1024]{2,1,0:T(1,128)S(1)}, f32[6,1,1024]{2,1,0:T(1,128)S(1)}, u32[]{:S(2)}, u32[]{:S(2)}) collective-permute-start(f32[6,1,1024]{2,1,0:T(1,128)S(1)} %get-tuple-element.173), channel_id=1, source_target_pairs={{0,1},{1,2},{2,3},{4,5},{5,6},{6,7},{8,9},{9,10},{10,11},{12,13},{... | collective-permute-start | bytes 73736 | tf_op jit(solution)/shard_map/ppermute | solution.py:21
  68.5 7.4 %while.34 = (s32[]{:T(128)}, f32[128]{0:T(128)S(1)}, f32[4,8192]{1,0:T(4,128)S(1)}, s32[4,8192]{1,0:T(4,128)S(1)}, s32[]{:T(128)}, /*index=5*/s32[]{:T(128)}) while((s32[]{:T(128)}, f32[128]{0:T(128)S(1)}, f32[4,8192]{1,0:T(4,128)S(1)}, s32[4,8192]{1,0:T(4,128)S(1)}, s32[]{:T(128)}, /*index=5*/s32[]{:T(128)}) %tuple.89), condition=%wide.region_5.6_spmd.clone, body=%wide.region_4.5_spmd.clone.sunk | while | flops 13631747 | bytes 132183 | solution.py:71
  68.6 1.8 fusion.120
  70.4 1.8 fusion.120
  72.3 1.8 fusion.120
  74.2 1.8 fusion.120
  76.0 32.0 %psum.22 = f32[128]{0:T(128)S(1)} all-reduce(f32[128]{0:T(128)S(1)} %get-tuple-element.84), channel_id=1, replica_groups=mesh['parts'=2,'gx'=4,'gy'=4] {'gx','gy'}, use_global_device_ids=true, to_apply=%region_6.7 | all-reduce | flops 128 | bytes 1024 | tf_op jit(solution)/shard_map/psum | solution.py:110
  112.5 3.0 %collective-permute-start.9 = (f32[1,8,1024]{2,1,0:T(8,128)S(1)}, f32[1,8,1024]{2,1,0:T(8,128)S(1)}, u32[]{:S(2)}, u32[]{:S(2)}) collective-permute-start(f32[1,8,1024]{2,1,0:T(8,128)S(1)} %get-tuple-element.178), channel_id=1, source_target_pairs={{0,4},{4,8},{8,12},{1,5},{5,9},{9,13},{2,6},{6,10},{10,14},{3,7},{... | collective-permute-start | bytes 98312 | tf_op jit(solution)/shard_map/ppermute | solution.py:21
  117.7 4.5 %collective-permute-start.11 = (f32[6,1,1024]{2,1,0:T(1,128)S(1)}, f32[6,1,1024]{2,1,0:T(1,128)S(1)}, u32[]{:S(2)}, u32[]{:S(2)}) collective-permute-start(f32[6,1,1024]{2,1,0:T(1,128)S(1)} %get-tuple-element.171), channel_id=1, source_target_pairs={{0,1},{1,2},{2,3},{4,5},{5,6},{6,7},{8,9},{9,10},{10,11},{12,13},{... | collective-permute-start | bytes 73736 | tf_op jit(solution)/shard_map/ppermute | solution.py:21
  124.2 7.4 %while.35 = (s32[]{:T(128)}, f32[128]{0:T(128)S(1)}, f32[4,8192]{1,0:T(4,128)S(1)}, s32[4,8192]{1,0:T(4,128)S(1)}, s32[]{:T(128)}, /*index=5*/s32[]{:T(128)}) while((s32[]{:T(128)}, f32[128]{0:T(128)S(1)}, f32[4,8192]{1,0:T(4,128)S(1)}, s32[4,8192]{1,0:T(4,128)S(1)}, s32[]{:T(128)}, /*index=5*/s32[]{:T(128)}) %tuple.87), condition=%wide.region_9.10_spmd.clone, body=%wide.region_8.9_spmd.clone.sunk | while | flops 13631747 | bytes 132183 | solution.py:71
  126.1 1.8 fusion.122
  128.0 1.8 fusion.122
  131.6 32.0 %psum.23 = f32[128]{0:T(128)S(1)} all-reduce(f32[128]{0:T(128)S(1)} %get-tuple-element.85), channel_id=1, replica_groups=mesh['parts'=2,'gx'=4,'gy'=4] {'gx','gy'}, use_global_device_ids=true, to_apply=%region_10.11 | all-reduce | flops 128 | bytes 1024 | tf_op jit(solution)/shard_map/psum | solution.py:110
  175.3 3.0 %collective-permute-start.13 = (f32[1,8,1024]{2,1,0:T(8,128)S(1)}, f32[1,8,1024]{2,1,0:T(8,128)S(1)}, u32[]{:S(2)}, u32[]{:S(2)}) collective-permute-start(f32[1,8,1024]{2,1,0:T(8,128)S(1)} %get-tuple-element.176), channel_id=1, source_target_pairs={{0,4},{4,8},{8,12},{1,5},{5,9},{9,13},{2,6},{6,10},{10,14},{3,7},{... | collective-permute-start | bytes 98312 | tf_op jit(solution)/shard_map/ppermute | solution.py:21
  180.5 4.5 %collective-permute-start.15 = (f32[6,1,1024]{2,1,0:T(1,128)S(1)}, f32[6,1,1024]{2,1,0:T(1,128)S(1)}, u32[]{:S(2)}, u32[]{:S(2)}) collective-permute-start(f32[6,1,1024]{2,1,0:T(1,128)S(1)} %get-tuple-element.169), channel_id=1, source_target_pairs={{0,1},{1,2},{2,3},{4,5},{5,6},{6,7},{8,9},{9,10},{10,11},{12,13},{... | collective-permute-start | bytes 73736 | tf_op jit(solution)/shard_map/ppermute | solution.py:21
  (90 shorter events, 31.5 us)
Async XLA Ops:
  0.6 1.1 copy-start
  0.7 1.1 copy-start.2
  45.8 4.5 %copy-start.4 = (s32[4,8,1024]{2,1,0:T(8,128)S(1)}, s32[4,8,1024]{2,1,0:T(8,128)}, u32[]{:S(2)}) copy-start(s32[4,8,1024]{2,1,0:T(8,128)} %param.13) | copy-start | bytes 393220
  45.8 4.5 %copy-start.3 = (f32[4,8,1024]{2,1,0:T(8,128)S(1)}, f32[4,8,1024]{2,1,0:T(8,128)}, u32[]{:S(2)}) copy-start(f32[4,8,1024]{2,1,0:T(8,128)} %param.12) | copy-start | bytes 393220
  45.8 8.9 %collective-permute-start.1 = (f32[1,8,1024]{2,1,0:T(8,128)S(1)}, f32[1,8,1024]{2,1,0:T(8,128)S(1)}, u32[]{:S(2)}, u32[]{:S(2)}) collective-permute-start(f32[1,8,1024]{2,1,0:T(8,128)S(1)} %get-tuple-element.183), channel_id=1, source_target_pairs={{4,0},{8,4},{12,8},{5,1},{9,5},{13,9},{6,2},{10,6},{14,10},{7,3},{... | collective-permute-start | bytes 98312 | tf_op jit(solution)/shard_map/ppermute | solution.py:24
  47.3 7.5 %collective-permute-start.3 = (f32[1,8,1024]{2,1,0:T(8,128)S(1)}, f32[1,8,1024]{2,1,0:T(8,128)S(1)}, u32[]{:S(2)}, u32[]{:S(2)}) collective-permute-start(f32[1,8,1024]{2,1,0:T(8,128)S(1)} %get-tuple-element.182), channel_id=1, source_target_pairs={{0,4},{4,8},{8,12},{1,5},{5,9},{9,13},{2,6},{6,10},{10,14},{3,7},{... | collective-permute-start | bytes 98312 | tf_op jit(solution)/shard_map/ppermute | solution.py:21
  50.4 10.3 %collective-permute-start = (f32[1,8,1024]{2,1,0:T(8,128)S(1)}, f32[1,8,1024]{2,1,0:T(8,128)S(1)}, u32[]{:S(2)}, u32[]{:S(2)}) collective-permute-start(f32[1,8,1024]{2,1,0:T(8,128)S(1)} %get-tuple-element.181), channel_id=1, source_target_pairs={{4,0},{8,4},{12,8},{5,1},{9,5},{13,9},{6,2},{10,6},{14,10},{7,3},{... | collective-permute-start | bytes 98312 | tf_op jit(solution)/shard_map/ppermute | solution.py:24
  51.7 9.0 %collective-permute-start.2 = (f32[1,8,1024]{2,1,0:T(8,128)S(1)}, f32[1,8,1024]{2,1,0:T(8,128)S(1)}, u32[]{:S(2)}, u32[]{:S(2)}) collective-permute-start(f32[1,8,1024]{2,1,0:T(8,128)S(1)} %get-tuple-element.180), channel_id=1, source_target_pairs={{0,4},{4,8},{8,12},{1,5},{5,9},{9,13},{2,6},{6,10},{10,14},{3,7},{... | collective-permute-start | bytes 98312 | tf_op jit(solution)/shard_map/ppermute | solution.py:21
  54.8 11.8 %collective-permute-start.5 = (f32[6,1,1024]{2,1,0:T(1,128)S(1)}, f32[6,1,1024]{2,1,0:T(1,128)S(1)}, u32[]{:S(2)}, u32[]{:S(2)}) collective-permute-start(f32[6,1,1024]{2,1,0:T(1,128)S(1)} %get-tuple-element.174), channel_id=1, source_target_pairs={{1,0},{2,1},{3,2},{5,4},{6,5},{7,6},{9,8},{10,9},{11,10},{13,12},{... | collective-permute-start | bytes 73736 | tf_op jit(solution)/shard_map/ppermute | solution.py:24
  56.1 10.5 %collective-permute-start.7 = (f32[6,1,1024]{2,1,0:T(1,128)S(1)}, f32[6,1,1024]{2,1,0:T(1,128)S(1)}, u32[]{:S(2)}, u32[]{:S(2)}) collective-permute-start(f32[6,1,1024]{2,1,0:T(1,128)S(1)} %get-tuple-element.175), channel_id=1, source_target_pairs={{0,1},{1,2},{2,3},{4,5},{5,6},{6,7},{8,9},{9,10},{10,11},{12,13},{... | collective-permute-start | bytes 73736 | tf_op jit(solution)/shard_map/ppermute | solution.py:21
  60.7 5.9 %collective-permute-start.4 = (f32[6,1,1024]{2,1,0:T(1,128)S(1)}, f32[6,1,1024]{2,1,0:T(1,128)S(1)}, u32[]{:S(2)}, u32[]{:S(2)}) collective-permute-start(f32[6,1,1024]{2,1,0:T(1,128)S(1)} %get-tuple-element.172), channel_id=1, source_target_pairs={{1,0},{2,1},{3,2},{5,4},{6,5},{7,6},{9,8},{10,9},{11,10},{13,12},{... | collective-permute-start | bytes 73736 | tf_op jit(solution)/shard_map/ppermute | solution.py:24
  62.0 6.1 %collective-permute-start.6 = (f32[6,1,1024]{2,1,0:T(1,128)S(1)}, f32[6,1,1024]{2,1,0:T(1,128)S(1)}, u32[]{:S(2)}, u32[]{:S(2)}) collective-permute-start(f32[6,1,1024]{2,1,0:T(1,128)S(1)} %get-tuple-element.173), channel_id=1, source_target_pairs={{0,1},{1,2},{2,3},{4,5},{5,6},{6,7},{8,9},{9,10},{10,11},{12,13},{... | collective-permute-start | bytes 73736 | tf_op jit(solution)/shard_map/ppermute | solution.py:21
  111.2 5.0 %collective-permute-start.8 = (f32[1,8,1024]{2,1,0:T(8,128)S(1)}, f32[1,8,1024]{2,1,0:T(8,128)S(1)}, u32[]{:S(2)}, u32[]{:S(2)}) collective-permute-start(f32[1,8,1024]{2,1,0:T(8,128)S(1)} %get-tuple-element.179), channel_id=1, source_target_pairs={{4,0},{8,4},{12,8},{5,1},{9,5},{13,9},{6,2},{10,6},{14,10},{7,3},{... | collective-permute-start | bytes 98312 | tf_op jit(solution)/shard_map/ppermute | solution.py:24
  112.5 3.9 %collective-permute-start.9 = (f32[1,8,1024]{2,1,0:T(8,128)S(1)}, f32[1,8,1024]{2,1,0:T(8,128)S(1)}, u32[]{:S(2)}, u32[]{:S(2)}) collective-permute-start(f32[1,8,1024]{2,1,0:T(8,128)S(1)} %get-tuple-element.178), channel_id=1, source_target_pairs={{0,4},{4,8},{8,12},{1,5},{5,9},{9,13},{2,6},{6,10},{10,14},{3,7},{... | collective-permute-start | bytes 98312 | tf_op jit(solution)/shard_map/ppermute | solution.py:21
  116.4 6.6 %collective-permute-start.10 = (f32[6,1,1024]{2,1,0:T(1,128)S(1)}, f32[6,1,1024]{2,1,0:T(1,128)S(1)}, u32[]{:S(2)}, u32[]{:S(2)}) collective-permute-start(f32[6,1,1024]{2,1,0:T(1,128)S(1)} %get-tuple-element.170), channel_id=1, source_target_pairs={{1,0},{2,1},{3,2},{5,4},{6,5},{7,6},{9,8},{10,9},{11,10},{13,12},{... | collective-permute-start | bytes 73736 | tf_op jit(solution)/shard_map/ppermute | solution.py:24
  117.7 6.1 %collective-permute-start.11 = (f32[6,1,1024]{2,1,0:T(1,128)S(1)}, f32[6,1,1024]{2,1,0:T(1,128)S(1)}, u32[]{:S(2)}, u32[]{:S(2)}) collective-permute-start(f32[6,1,1024]{2,1,0:T(1,128)S(1)} %get-tuple-element.171), channel_id=1, source_target_pairs={{0,1},{1,2},{2,3},{4,5},{5,6},{6,7},{8,9},{9,10},{10,11},{12,13},{... | collective-permute-start | bytes 73736 | tf_op jit(solution)/shard_map/ppermute | solution.py:21
  173.9 12.6 %copy-start.1 = (f32[4,8,1024]{2,1,0:T(8,128)}, f32[4,8,1024]{2,1,0:T(8,128)S(1)}, u32[]{:S(2)}) copy-start(f32[4,8,1024]{2,1,0:T(8,128)S(1)} %multiply_add_fusion) | copy-start | bytes 393220
  174.0 4.3 %collective-permute-start.12 = (f32[1,8,1024]{2,1,0:T(8,128)S(1)}, f32[1,8,1024]{2,1,0:T(8,128)S(1)}, u32[]{:S(2)}, u32[]{:S(2)}) collective-permute-start(f32[1,8,1024]{2,1,0:T(8,128)S(1)} %get-tuple-element.177), channel_id=1, source_target_pairs={{4,0},{8,4},{12,8},{5,1},{9,5},{13,9},{6,2},{10,6},{14,10},{7,3},{... | collective-permute-start | bytes 98312 | tf_op jit(solution)/shard_map/ppermute | solution.py:24
  175.3 3.9 %collective-permute-start.13 = (f32[1,8,1024]{2,1,0:T(8,128)S(1)}, f32[1,8,1024]{2,1,0:T(8,128)S(1)}, u32[]{:S(2)}, u32[]{:S(2)}) collective-permute-start(f32[1,8,1024]{2,1,0:T(8,128)S(1)} %get-tuple-element.176), channel_id=1, source_target_pairs={{0,4},{4,8},{8,12},{1,5},{5,9},{9,13},{2,6},{6,10},{10,14},{3,7},{... | collective-permute-start | bytes 98312 | tf_op jit(solution)/shard_map/ppermute | solution.py:21
  179.2 5.9 %collective-permute-start.14 = (f32[6,1,1024]{2,1,0:T(1,128)S(1)}, f32[6,1,1024]{2,1,0:T(1,128)S(1)}, u32[]{:S(2)}, u32[]{:S(2)}) collective-permute-start(f32[6,1,1024]{2,1,0:T(1,128)S(1)} %get-tuple-element.168), channel_id=1, source_target_pairs={{1,0},{2,1},{3,2},{5,4},{6,5},{7,6},{9,8},{10,9},{11,10},{13,12},{... | collective-permute-start | bytes 73736 | tf_op jit(solution)/shard_map/ppermute | solution.py:24
  180.5 6.1 %collective-permute-start.15 = (f32[6,1,1024]{2,1,0:T(1,128)S(1)}, f32[6,1,1024]{2,1,0:T(1,128)S(1)}, u32[]{:S(2)}, u32[]{:S(2)}) collective-permute-start(f32[6,1,1024]{2,1,0:T(1,128)S(1)} %get-tuple-element.169), channel_id=1, source_target_pairs={{0,1},{1,2},{2,3},{4,5},{5,6},{6,7},{8,9},{9,10},{10,11},{12,13},{... | collective-permute-start | bytes 73736 | tf_op jit(solution)/shard_map/ppermute | solution.py:21
where the time goes:
time: 191 us; the launch traced here: 188 us
  blocking collectives  99.1 us (52%)
  starting transfers between devices  40.8 us (21%)
  matrix products  22.6 us (12%)
  other arithmetic  8.73 us (5%)
  between operations  8.21 us (4%)
  waiting for transfers between devices  4.75 us (2%)
  local copies, waits for them, and re-layouts  2.96 us (2%)
    psum x3, blocking collectives, sketch_sum(): lax.psum(sketch_local(field, compressed_slot_number, normal_draw_factor),...  99.1 us
    ppermute x8, starting transfers between devices, padded_2(): lax.ppermute(lax.slice_in_dim(block, block.shape[dim] - width, None, axis...  30.3 us
    dot_general x12, matrix products, add_block(): return (totals + jnp.dot(block_vals, onehot, precision=highest), None)  21.6 us
    ppermute x8, starting transfers between devices, padded_2(): lax.ppermute(lax.slice_in_dim(block, 0, width, axis=dim), axis, backward)  10.5 us
    ppermute x8, waiting for transfers between devices, padded_2(): lax.ppermute(lax.slice_in_dim(block, block.shape[dim] - width, None, axis...  4.73 us
  transfers between devices with their start and end apart: 16, of which 5 were waited for; matrix products, arithmetic and copies ran while one was open for 1% of the time, Pallas kernels for 0%

commit v1 on v0

v1 whole, which is shorter than its diff:
```python
import functools

import jax
import jax.numpy as jnp
from jax import lax
from jax.experimental import pallas as pl
from jax.experimental.pallas import tpu as pltpu
from jax.sharding import PartitionSpec as P

SKETCH = 128
FIELDS = 3
LANES = 128
epsilon = 1e-06
roomy = pltpu.CompilerParams(vmem_limit_bytes=48 * 1024 * 1024)


def traits(warmth, phase):
    powder, solid = phase == 0, phase == 1
    offset = jnp.where(powder, 0.2, jnp.where(solid, 1.0, 0.6))
    return offset * (0.5 + warmth), jnp.where(powder, 1.0, jnp.where(solid, 2.0, 1.5))


def link(first, second):
    total = first + second
    return 2.0 * first * second / jnp.where(total > 0.0, total, 1.0)


def ahead(plane, axis):
    return pltpu.roll(plane, plane.shape[axis] - 1, axis)


def inner_links(cond):
    links = []
    for axis in (0, 1):
        index = lax.broadcasted_iota(jnp.int32, cond.shape, axis)
        links.append(
            jnp.where(index < cond.shape[axis] - 1, link(cond, ahead(cond, axis)), 0.0)
        )
    return links


def inner_flow(field, links):
    total = None
    for axis in (0, 1):
        flow = links[axis] * (field - ahead(field, axis))
        part = flow - pltpu.roll(flow, 1, axis)
        total = part if total is None else total + part
    return total


def first_kernel(b_ref, warmth_ref, phase_ref, cond_ref, inner_ref, down_ref, up_ref):
    planes = b_ref.shape[0]
    images, conds, before = [], [], None
    for i in range(planes):
        cond, cap = traits(warmth_ref[i], phase_ref[i])
        field = b_ref[i]
        image = cap * field + inner_flow(field, inner_links(cond))
        if i:
            flow = link(conds[-1], cond) * (b_ref[i - 1] - field)
            images[-1] = images[-1] + flow
            image = image - flow
        conds.append(cond)
        images.append(image)
    for i in range(planes):
        cond_ref[i] = conds[i]
        inner_ref[i] = images[i]
    for ref, i in ((down_ref, 0), (up_ref, planes - 1)):
        ref[0] = images[i]
        ref[1] = b_ref[i]
        ref[2] = conds[i]


def second_kernel(b_ref, cond_ref, inner_ref, low_ref, high_ref, wide_ref, down_ref, up_ref):
    planes, rows = b_ref.shape[0], b_ref.shape[1]
    low_flow = link(low_ref[2], cond_ref[0]) * (low_ref[1] - b_ref[0])
    high_flow = link(cond_ref[planes - 1], high_ref[2]) * (b_ref[planes - 1] - high_ref[1])
    images = [low_ref[0] + low_flow] + [inner_ref[i] for i in range(planes)]
    images.append(high_ref[0] - high_flow)
    images[1] = images[1] - low_flow
    images[planes] = images[planes] + high_flow
    for i in range(planes + 2):
        wide_ref[i] = images[i]
    for ref, row in ((down_ref, 0), (up_ref, rows - 1)):
        at = slice(row, row + 1)
        for i in range(planes):
            ref[i : i + 1] = images[i + 1][at]
        for base, own, which in ((planes, b_ref, 1), (2 * planes + 2, cond_ref, 2)):
            ref[base : base + 1] = low_ref[which, at]
            for i in range(planes):
                ref[base + 1 + i : base + 2 + i] = own[i, at]
            ref[base + planes + 1 : base + planes + 2] = high_ref[which, at]


def third_kernel(
    b_ref, cond_ref, phase_ref, slot_ref, draw_ref, wide_ref, xlow_ref, xhigh_ref, ylow_ref,
    yhigh_ref, image_ref, twice_ref, sketch_ref, cells_ref,
):
    planes, rows, depth = b_ref.shape
    index = lax.broadcasted_iota(jnp.int32, (rows, depth), 0)
    first, last = index == 0, index == rows - 1

    b_wide = [xlow_ref[1]] + [b_ref[i] for i in range(planes)] + [xhigh_ref[1]]
    c_wide = [xlow_ref[2]] + [cond_ref[i] for i in range(planes)] + [xhigh_ref[2]]
    images, edge_links, edge_values = [], [], []
    for i in range(planes + 2):
        image = wide_ref[i]
        links, values = [], []
        for ref, mask in ((ylow_ref, first), (yhigh_ref, last)):
            base = planes + i
            b_side = jnp.broadcast_to(ref[base : base + 1], (rows, depth))
            base = 2 * planes + 2 + i
            c_side = jnp.broadcast_to(ref[base : base + 1], (rows, depth))
            conductance = jnp.where(mask, link(c_wide[i], c_side), 0.0)
            flow = conductance * (b_wide[i] - b_side)
            image = image + flow
            if 0 < i <= planes:
                beyond = jnp.broadcast_to(ref[i - 1 : i], (rows, depth))
                values.append(beyond - flow)
                links.append(conductance)
        images.append(image)
        edge_links.append(links)
        edge_values.append(values)

    flow_low = link(c_wide[0], c_wide[1]) * (images[0] - images[1])
    for i in range(1, planes + 1):
        unused, cap = traits(0.0, phase_ref[i - 1])
        image = images[i]
        flow = link(c_wide[i], c_wide[i + 1]) * (image - images[i + 1])
        twice = cap * image + inner_flow(image, inner_links(c_wide[i])) + (flow - flow_low)
        flow_low = flow
        for conductance, value in zip(edge_links[i], edge_values[i]):
            twice = twice + conductance * (image - value)
        image_ref[i - 1] = image
        twice_ref[i - 1] = twice
        draw = draw_ref[i - 1]
        for f, field in enumerate((b_wide[i], image, twice)):
            weighted = draw * field
            for t in range(depth // LANES):
                cells_ref[t, pl.ds((i - 1) * rows * 8 + f, rows, stride=8), :] = weighted[
                    :, t * LANES : (t + 1) * LANES
                ]

    slots = lax.broadcasted_iota(jnp.int32, (SKETCH, depth), 0).astype(jnp.float32)
    slots = slots.astype(jnp.bfloat16)
    one = jnp.ones((SKETCH, depth), jnp.bfloat16)
    used = lax.broadcasted_iota(jnp.int32, (8, depth), 0) < FIELDS

    def add_row(r, total):
        at = pl.ds(pl.multiple_of(r * 8, 8), 8)
        cells = [cells_ref[t, at, :] for t in range(depth // LANES)]
        cells = jnp.where(used, jnp.concatenate(cells, axis=1), 0.0)
        coarse = cells.astype(jnp.bfloat16)
        fine = (cells - coarse.astype(jnp.float32)).astype(jnp.bfloat16)
        both = jnp.concatenate([coarse, fine], axis=0)
        ids = slot_ref[pl.ds(r, 1), :].astype(jnp.float32)
        ids = jnp.broadcast_to(ids, (SKETCH, depth)).astype(jnp.bfloat16)
        chosen = jnp.where(ids == slots, one, jnp.zeros_like(one))
        return total + lax.dot_general(
            both, chosen, (((1,), (1,)), ((), ())), preferred_element_type=jnp.float32
        )

    total = lax.fori_loop(
        0, planes * rows, add_row, jnp.zeros((16, SKETCH), jnp.float32), unroll=4
    )
    sketch_ref[...] = total[:8] + total[8:]


def last_kernel(sketch_ref, b_ref, image_ref, twice_ref, solution_ref, residual_ref):
    sketches = jnp.sum(sketch_ref[...], axis=0)

    def inner(first, second):
        return jnp.sum(first * second, axis=1, keepdims=True)

    s0, s1, s2 = (sketches[i : i + 1] for i in range(FIELDS))
    beta = jnp.sqrt(inner(s0, s0) + epsilon)
    q0 = s0 / beta
    p0 = s1 / beta
    h00 = inner(q0, p0)
    t0 = p0 - h00 * q0
    n0 = jnp.sqrt(inner(t0, t0) + epsilon)
    q1 = t0 / n0
    p1 = (s2 / beta - h00 * p0) / n0
    h01 = inner(q0, p1)
    h11 = inner(q1, p1)
    t1 = p1 - h01 * q0 - h11 * q1
    n1 = jnp.sqrt(inner(t1, t1) + epsilon)
    l00 = jnp.sqrt(h00 * h00 + n0 * n0)
    l10 = (h00 * h01 + n0 * h11) / l00
    l11 = jnp.sqrt(h01 * h01 + h11 * h11 + n1 * n1 - l10 * l10)
    z0 = beta * h00 / l00
    z1 = (beta * h01 - l10 * z0) / l11
    y1 = z1 / l11
    y0 = (z0 - l10 * y1) / l00
    c1 = y1 / (beta * n0)
    c0 = y0 / beta - h00 * c1
    for i in range(b_ref.shape[0]):
        b, image = b_ref[i], image_ref[i]
        solution_ref[i] = c0 * b + c1 * image
        residual_ref[i] = b - c0 * image - c1 * twice_ref[i]


def call(kernel, shapes, *operands, scratch=()):
    vmem = pl.BlockSpec(memory_space=pltpu.VMEM)
    return pl.pallas_call(
        kernel,
        out_shape=[jax.ShapeDtypeStruct(shape, jnp.float32) for shape in shapes],
        in_specs=[vmem] * len(operands),
        out_specs=[vmem] * len(shapes),
        scratch_shapes=scratch,
        compiler_params=roomy,
    )(*operands)


def swap(down, up, axis):
    count = lax.axis_size(axis)
    forward = [(i, i + 1) for i in range(count - 1)]
    backward = [(i + 1, i) for i in range(count - 1)]
    return lax.ppermute(up, axis, forward), lax.ppermute(down, axis, backward)


def everyones(sketch):
    count = lax.axis_size("gx") * lax.axis_size("gy")
    copies = jnp.broadcast_to(sketch[None], (count,) + sketch.shape)
    return lax.all_to_all(copies, ("gx", "gy"), 0, 0)


def body(b, warmth, phase, slots, draw):
    planes, rows, depth = b.shape
    block, plane, wide = b.shape, (3, rows, depth), (planes + 2, rows, depth)
    line = (3 * planes + 4, depth)
    cond, inner, down, up = call(first_kernel, [block, block, plane, plane], b, warmth, phase)
    xlow, xhigh = swap(down, up, "gx")
    image_wide, down, up = call(
        second_kernel, [wide, line, line], b, cond, inner, xlow, xhigh
    )
    ylow, yhigh = swap(down, up, "gy")
    image, twice, sketch = call(
        third_kernel,
        [block, block, (8, SKETCH)],
        b, cond, phase, slots.reshape(planes * rows, depth), draw, image_wide, xlow, xhigh,
        ylow, yhigh,
        scratch=[pltpu.VMEM((depth // LANES, planes * rows * 8, LANES), jnp.float32)],
    )
    return tuple(call(last_kernel, [block, block], everyones(sketch), b, image, twice))


def solution(mesh):
    spec = P(("parts", "gx"), "gy", None)
    return jax.shard_map(
        body, mesh=mesh, in_specs=(spec,) * 5, out_specs=(spec,) * 2, check_vma=False
    )
```

time: 191 us -> 39.2 us (0.21); the launches traced: 188 us -> 38.9 us
  blocking collectives: 99.1 us -> 12.9 us
  starting transfers between devices: 40.8 us -> 8.56 us
  matrix products: 22.6 us -> 0 us
  other arithmetic: 8.73 us -> 0 us
  between operations: 8.21 us -> 0.71 us
  Pallas kernels: 0 us -> 5.14 us
  waiting for transfers between devices: 4.75 us -> 8.88 us
    psum x3 -> x0, blocking collectives: 99.1 us -> none  [sketch_sum(): lax.psum(sketch_local(field, compressed_slot_number, normal_draw_factor),...]
    ppermute x16 -> x4, starting transfers between devices: 40.8 us -> 8.56 us  [swap(): return (lax.ppermute(up, axis, forward), lax.ppermute(down, axis, backward))]
    dot_general x15 -> x0, matrix products: 22.6 us -> none  [the longest x12 21.6 us: add_block(): return (totals + jnp.dot(block_vals, onehot, precision=highest), None)]
    all_to_all x0 -> x1, blocking collectives: none -> 12.9 us  [everyones(): return lax.all_to_all(copies, ('gx', 'gy'), 0, 0)]
    pallas_call x0 -> x4, Pallas kernels: none -> 5.14 us  [call(): pl.pallas_call(kernel, out_shape=[jax.ShapeDtypeStruct(shape, jnp.float32...]
    ppermute x16 -> x4, waiting for transfers between devices: 4.75 us -> 8.88 us  [swap(): return (lax.ppermute(up, axis, forward), lax.ppermute(down, axis, backward))]
    another operation x7 -> x0, other arithmetic: 2.32 us -> none  [the longest x3 0.86 us: solve_small(): factor = jnp.linalg.cholesky(gram_matrix)]
  transfers between devices with their start and end apart: 16 -> 4, of which waited for: 5 -> 3; matrix products, arithmetic and copies ran while one was open for 1% -> 0% of each run, Pallas kernels for 0% -> 0%
where the time goes in v1:
time: 39.2 us; the launch traced here: 38.9 us
  blocking collectives  12.9 us (33%)
  waiting for transfers between devices  8.88 us (23%)
  starting transfers between devices  8.56 us (22%)
  Pallas kernels  5.14 us (13%)
  local copies, waits for them, and re-layouts  2.73 us (7%)
  between operations  0.71 us (2%)
    all_to_all x1, blocking collectives, everyones(): return lax.all_to_all(copies, ('gx', 'gy'), 0, 0)  12.9 us
    ppermute x4, waiting for transfers between devices, swap(): return (lax.ppermute(up, axis, forward), lax.ppermute(down, axis, backward))  8.88 us
    ppermute x4, starting transfers between devices, swap(): return (lax.ppermute(up, axis, forward), lax.ppermute(down, axis, backward))  8.56 us
    pallas_call x4, Pallas kernels, call(): pl.pallas_call(kernel, out_shape=[jax.ShapeDtypeStruct(shape, jnp.float32...  5.14 us
    unnamed x12, local copies, waits for them, and re-layouts  2.72 us
  transfers between devices with their start and end apart: 4, of which 3 were waited for; matrix products, arithmetic and copies ran while one was open for 0% of the time, Pallas kernels for 0%

profile of v1, /device:TPU:0, one launch (start us, length us, event | category | flops | bytes accessed | tf_op | source)
XLA Modules:
  0.0 38.9 jit_solution(16719742007229588107)
XLA Ops:
  0.6 0.0 copy-start
  0.6 0.9 %copy-done = f32[4,8,1024]{2,1,0:T(8,128)S(1)} copy-done((f32[4,8,1024]{2,1,0:T(8,128)S(1)}, f32[4,8,1024]{2,1,0:T(8,128)}, u32[]{:S(2)}) %copy-start) | copy-done | bytes 131096
  1.5 0.0 copy-start.1
  1.5 0.9 %copy-done.1 = s32[4,8,1024]{2,1,0:T(8,128)S(1)} copy-done((s32[4,8,1024]{2,1,0:T(8,128)S(1)}, s32[4,8,1024]{2,1,0:T(8,128)}, u32[]{:S(2)}) %copy-start.1) | copy-done | bytes 131096
  2.4 0.0 copy-start.3
  2.4 0.9 %copy-done.3 = f32[4,8,1024]{2,1,0:T(8,128)S(1)} copy-done((f32[4,8,1024]{2,1,0:T(8,128)S(1)}, f32[4,8,1024]{2,1,0:T(8,128)}, u32[]{:S(2)}) %copy-start.3) | copy-done | bytes 131096
  3.3 0.2 shard_map.68
  3.6 2.4 %collective-permute-start = (f32[3,8,1024]{2,1,0:T(8,128)S(1)}, f32[3,8,1024]{2,1,0:T(8,128)S(1)}, u32[]{:S(2)}, u32[]{:S(2)}) collective-permute-start(f32[3,8,1024]{2,1,0:T(8,128)S(1)} %get-tuple-element.14), channel_id=1, source_target_pairs={{0,4},{4,8},{8,12},{1,5},{5,9},{9,13},{2,6},{6,10},{10,14},{3,7},{... | collective-permute-start | bytes 294920 | tf_op jit(solution)/shard_map/ppermute | solution.py:218
  6.0 1.3 %collective-permute-start.1 = (f32[3,8,1024]{2,1,0:T(8,128)S(1)}, f32[3,8,1024]{2,1,0:T(8,128)S(1)}, u32[]{:S(2)}, u32[]{:S(2)}) collective-permute-start(f32[3,8,1024]{2,1,0:T(8,128)S(1)} %get-tuple-element.15), channel_id=1, source_target_pairs={{4,0},{8,4},{12,8},{5,1},{9,5},{13,9},{6,2},{10,6},{14,10},{7,3},{... | collective-permute-start | bytes 294920 | tf_op jit(solution)/shard_map/ppermute | solution.py:218
  7.3 0.0 collective-permute-done.low_ref.xlow_ref
  7.3 4.0 %collective-permute-done.1.high_ref.xhigh_ref = f32[3,8,1024]{2,1,0:T(8,128)S(1)} collective-permute-done((f32[3,8,1024]{2,1,0:T(8,128)S(1)}, f32[3,8,1024]{2,1,0:T(8,128)S(1)}, u32[]{:S(2)}, u32[]{:S(2)}) %collective-permute-start.1) | collective-permute-done | bytes 98336 | tf_op jit(solution)/shard_map/ppermute | solution.py:218
  11.3 0.0 copy-start.2
  11.3 0.0 copy-start.4
  11.3 0.1 shard_map.69
  11.4 3.6 %collective-permute-start.2 = (f32[16,1024]{1,0:T(8,128)S(1)}, f32[16,1024]{1,0:T(8,128)S(1)}, u32[]{:S(2)}, u32[]{:S(2)}) collective-permute-start(f32[16,1024]{1,0:T(8,128)S(1)} %get-tuple-element.17), channel_id=1, source_target_pairs={{0,1},{1,2},{2,3},{4,5},{5,6},{6,7},{8,9},{9,10},{10,11},{12,13},{... | collective-permute-start | bytes 196616 | tf_op jit(solution)/shard_map/ppermute | solution.py:218
  15.0 1.3 %collective-permute-start.3 = (f32[16,1024]{1,0:T(8,128)S(1)}, f32[16,1024]{1,0:T(8,128)S(1)}, u32[]{:S(2)}, u32[]{:S(2)}) collective-permute-start(f32[16,1024]{1,0:T(8,128)S(1)} %get-tuple-element.18), channel_id=1, source_target_pairs={{1,0},{2,1},{3,2},{5,4},{6,5},{7,6},{9,8},{10,9},{11,10},{13,12},{... | collective-permute-start | bytes 196616 | tf_op jit(solution)/shard_map/ppermute | solution.py:218
  16.3 0.6 %collective-permute-done.2.ylow_ref = f32[16,1024]{1,0:T(8,128)S(1)} collective-permute-done((f32[16,1024]{1,0:T(8,128)S(1)}, f32[16,1024]{1,0:T(8,128)S(1)}, u32[]{:S(2)}, u32[]{:S(2)}) %collective-permute-start.2) | collective-permute-done | bytes 65568 | tf_op jit(solution)/shard_map/ppermute | solution.py:218
  16.9 4.3 %collective-permute-done.3.yhigh_ref = f32[16,1024]{1,0:T(8,128)S(1)} collective-permute-done((f32[16,1024]{1,0:T(8,128)S(1)}, f32[16,1024]{1,0:T(8,128)S(1)}, u32[]{:S(2)}, u32[]{:S(2)}) %collective-permute-start.3) | collective-permute-done | bytes 65568 | tf_op jit(solution)/shard_map/ppermute | solution.py:218
  21.1 0.0 copy-done.2
  21.1 0.0 copy-done.4
  21.1 0.0 copy-done.5
  21.2 3.6 %shard_map.70 = (f32[4,8,1024]{2,1,0:T(8,128)S(1)}, f32[4,8,1024]{2,1,0:T(8,128)S(1)}, f32[8,128]{1,0:T(8,128)S(1)}) custom-call(f32[4,8,1024]{2,1,0:T(8,128)S(1)} %copy-done, f32[4,8,1024]{2,1,0:T(8,128)S(1)} %get-tuple-element.12.cond_ref, s32[4,8,1024]{2,1,0:T(8,128)S(1)} %copy-done.2, s32[32,1024]{1,0:T(8,128)S(1)} %bitcast.1, ...), custom_call_target="tpu_custom_call" | custom-call | tf_op jit(solution)/shard_map/pallas_call | solution.py:204
  24.8 12.9 %all_to_all.5.sketch_ref = f32[16,8,128]{2,1,0:T(8,128)S(1)} all-to-all(f32[16,8,128]{2,1,0:T(8,128)S(1)} %broadcast_in_dim.2), channel_id=1, replica_groups=mesh['parts'=2,'gx'=4,'gy'=4] {'gx','gy'}, dimensions={0} | all-to-all | bytes 131072 | tf_op jit(solution)/shard_map/all_to_all | solution.py:224
  37.7 1.2 %shard_map.71 = (f32[4,8,1024]{2,1,0:T(8,128)}, f32[4,8,1024]{2,1,0:T(8,128)}) custom-call(f32[16,8,128]{2,1,0:T(8,128)S(1)} %all_to_all.5.sketch_ref, f32[4,8,1024]{2,1,0:T(8,128)S(1)} %copy-done, f32[4,8,1024]{2,1,0:T(8,128)S(1)} %get-tuple-element.20.image_ref, f32[4,8,1024]{2,1,0:T(8,128)S(1)} %get-tuple-element.21.twice_ref), custom_call_target="tpu_custom_call" | custom-call | tf_op jit(solution)/shard_map/pallas_call | solution.py:204
  (2 shorter events, 0.0 us)
Async XLA Ops:
  0.6 0.9 %copy-start = (f32[4,8,1024]{2,1,0:T(8,128)S(1)}, f32[4,8,1024]{2,1,0:T(8,128)}, u32[]{:S(2)}) copy-start(f32[4,8,1024]{2,1,0:T(8,128)} %b_ref.7) | copy-start | bytes 393220
  1.5 0.9 %copy-start.1 = (s32[4,8,1024]{2,1,0:T(8,128)S(1)}, s32[4,8,1024]{2,1,0:T(8,128)}, u32[]{:S(2)}) copy-start(s32[4,8,1024]{2,1,0:T(8,128)} %phase_ref.3) | copy-start | bytes 393220
  2.4 0.9 %copy-start.3 = (f32[4,8,1024]{2,1,0:T(8,128)S(1)}, f32[4,8,1024]{2,1,0:T(8,128)}, u32[]{:S(2)}) copy-start(f32[4,8,1024]{2,1,0:T(8,128)} %warmth_ref.1) | copy-start | bytes 393220
  3.6 3.7 %collective-permute-start = (f32[3,8,1024]{2,1,0:T(8,128)S(1)}, f32[3,8,1024]{2,1,0:T(8,128)S(1)}, u32[]{:S(2)}, u32[]{:S(2)}) collective-permute-start(f32[3,8,1024]{2,1,0:T(8,128)S(1)} %get-tuple-element.14), channel_id=1, source_target_pairs={{0,4},{4,8},{8,12},{1,5},{5,9},{9,13},{2,6},{6,10},{10,14},{3,7},{... | collective-permute-start | bytes 294920 | tf_op jit(solution)/shard_map/ppermute | solution.py:218
  6.0 5.3 %collective-permute-start.1 = (f32[3,8,1024]{2,1,0:T(8,128)S(1)}, f32[3,8,1024]{2,1,0:T(8,128)S(1)}, u32[]{:S(2)}, u32[]{:S(2)}) collective-permute-start(f32[3,8,1024]{2,1,0:T(8,128)S(1)} %get-tuple-element.15), channel_id=1, source_target_pairs={{4,0},{8,4},{12,8},{5,1},{9,5},{13,9},{6,2},{10,6},{14,10},{7,3},{... | collective-permute-start | bytes 294920 | tf_op jit(solution)/shard_map/ppermute | solution.py:218
  11.3 9.9 %copy-start.2 = (s32[4,8,1024]{2,1,0:T(8,128)S(1)}, s32[4,8,1024]{2,1,0:T(8,128)}, u32[]{:S(2)}) copy-start(s32[4,8,1024]{2,1,0:T(8,128)} %phase_ref.3) | copy-start | bytes 393220
  11.3 9.9 %copy-start.4 = (s32[4,8,1024]{2,1,0:T(8,128)S(1)}, s32[4,8,1024]{2,1,0:T(8,128)}, u32[]{:S(2)}) copy-start(s32[4,8,1024]{2,1,0:T(8,128)} %param.8) | copy-start | bytes 393220
  11.3 9.9 %copy-start.5 = (f32[4,8,1024]{2,1,0:T(8,128)S(1)}, f32[4,8,1024]{2,1,0:T(8,128)}, u32[]{:S(2)}) copy-start(f32[4,8,1024]{2,1,0:T(8,128)} %draw_ref.1) | copy-start | bytes 393220
  11.4 5.5 %collective-permute-start.2 = (f32[16,1024]{1,0:T(8,128)S(1)}, f32[16,1024]{1,0:T(8,128)S(1)}, u32[]{:S(2)}, u32[]{:S(2)}) collective-permute-start(f32[16,1024]{1,0:T(8,128)S(1)} %get-tuple-element.17), channel_id=1, source_target_pairs={{0,1},{1,2},{2,3},{4,5},{5,6},{6,7},{8,9},{9,10},{10,11},{12,13},{... | collective-permute-start | bytes 196616 | tf_op jit(solution)/shard_map/ppermute | solution.py:218
  15.0 6.2 %collective-permute-start.3 = (f32[16,1024]{1,0:T(8,128)S(1)}, f32[16,1024]{1,0:T(8,128)S(1)}, u32[]{:S(2)}, u32[]{:S(2)}) collective-permute-start(f32[16,1024]{1,0:T(8,128)S(1)} %get-tuple-element.18), channel_id=1, source_target_pairs={{1,0},{2,1},{3,2},{5,4},{6,5},{7,6},{9,8},{10,9},{11,10},{13,12},{... | collective-permute-start | bytes 196616 | tf_op jit(solution)/shard_map/ppermute | solution.py:218
